TPU v7x, 32 devices: a whole 2x2x4 slice. The times are simulated.
32 devices in a mesh: pairs: 2 (over x), tgt: 16 (over z, y, core).
Axes of the slice: x: 2, y: 2, z: 4, core: 2. Of those that a mesh axis runs over, the one named last changes fastest.
Arguments:
- src_hidden: bfloat16 [4096, 128], P(('pairs', 'tgt')), parts along dimension 0, may hold values from -6 to 6
- tgt_hidden: bfloat16 [256, 256, 128], P(('pairs', 'tgt')), parts along dimension 0, may hold values from -6 to 6
- proj_weight: bfloat16 [128, 256], replicated, may hold values from -0.5 to 0.5
- proj_bias: float32 [256], replicated, may hold values from -1.5 to 1.5
Outputs:
- level_one: bfloat16 [128, 128, 2048], P(('pairs', 'tgt')), parts along dimension 0
- level_two: bfloat16 [4096, 2048], P(('pairs', 'tgt')), parts along dimension 0
- level_three: bfloat16 [4096, 512], P(('pairs', 'tgt')), parts along dimension 0
There are 2 independent parts, one for each index of `pairs`. A program takes and returns all parts, laid end to end along the dimension named above; an argument that names none is the same for every part. Nothing has to cross between parts.
All inputs are finite; a program needn't handle non-finite values.
Results may differ from a plain program's by a relative error of at most 0.006.
Values may be sent and summed in bfloat16 or wider, within the bound.
A program may use at most 64 MiB of HBM per device.

v0:
```python
import math
import jax
import jax.numpy as jnp
from jax import lax
from jax.sharding import PartitionSpec as P


def project_features(hidden, weight, bias):
    result = jnp.dot(hidden, weight, preferred_element_type=jnp.float32) + bias
    return result.astype(jnp.bfloat16)


def pool_leading(values):
    height, across, depth = values.shape
    return values.reshape(height // 2, 2, across // 2, 2, depth).mean(axis=(1, 3))


def pool_trailing(values):
    depth, height, across = values.shape
    return values.reshape(depth, height // 2, 2, across // 2, 2).mean(axis=(2, 4))


def split_parts(values):
    upper = values.astype(jnp.bfloat16)
    lower = (values - upper.astype(jnp.float32)).astype(jnp.bfloat16)
    return (upper, lower)


def per_device(src_hidden, tgt_hidden, proj_weight, proj_bias):
    row_count, col_count, hidden_width = tgt_hidden.shape
    channels = proj_weight.shape[1]
    stripe_count = lax.axis_size("tgt")
    own_sources = src_hidden.shape[0]
    source_count = own_sources * stripe_count
    inverse_root = 1.0 / math.sqrt(channels)
    tgt_feat = project_features(
        tgt_hidden.reshape(row_count * col_count, hidden_width), proj_weight, proj_bias
    )
    grid_feat = tgt_feat.astype(jnp.float32).reshape(row_count, col_count, channels)
    fine_pool = pool_leading(grid_feat)
    coarse_pool = pool_leading(fine_pool)
    fine_upper, fine_lower = split_parts(fine_pool.reshape(-1, channels))
    coarse_upper, coarse_lower = split_parts(coarse_pool.reshape(-1, channels))
    own_features = project_features(src_hidden, proj_weight, proj_bias)
    all_features = lax.all_gather(own_features, "tgt", axis=0, tiled=True)
    block_size = 512
    block_total = source_count // block_size
    fine_count = fine_upper.shape[0]
    coarse_count = coarse_upper.shape[0]
    empty_levels = (
        jnp.zeros((fine_count, source_count), jnp.bfloat16),
        jnp.zeros((source_count, coarse_count), jnp.bfloat16),
    )
    contract_last = (((1,), (1,)), ((), ()))

    def one_block(block_index, levels):
        level_one, coarse_rows = levels
        offset = (block_index * block_size).astype(jnp.int32)
        panel = lax.dynamic_slice_in_dim(all_features, offset, block_size, 0)
        fine_corr = lax.dot_general(
            fine_upper, panel, contract_last, preferred_element_type=jnp.float32
        )
        fine_corr = fine_corr + lax.dot_general(
            fine_lower, panel, contract_last, preferred_element_type=jnp.float32
        )
        coarse_corr = lax.dot_general(
            panel, coarse_upper, contract_last, preferred_element_type=jnp.float32
        )
        coarse_corr = coarse_corr + lax.dot_general(
            panel, coarse_lower, contract_last, preferred_element_type=jnp.float32
        )
        zero_index = jnp.zeros((), jnp.int32)
        level_one = lax.dynamic_update_slice(
            level_one, (fine_corr * inverse_root).astype(jnp.bfloat16), (zero_index, offset)
        )
        coarse_rows = lax.dynamic_update_slice(
            coarse_rows, (coarse_corr * inverse_root).astype(jnp.bfloat16), (offset, zero_index)
        )
        return (level_one, coarse_rows)

    level_one, coarse_rows = lax.fori_loop(0, block_total, one_block, empty_levels)
    level_one = level_one.reshape(row_count // 2, col_count // 2, source_count)
    level_two = lax.all_to_all(coarse_rows, "tgt", split_axis=0, concat_axis=1, tiled=True)
    coarse_grid = level_two.astype(jnp.float32).reshape(
        own_sources, stripe_count * (row_count // 4), col_count // 4
    )
    level_three = pool_trailing(coarse_grid).reshape(own_sources, -1).astype(jnp.bfloat16)
    return (level_one, level_two, level_three)


def solution(mesh):
    return jax.shard_map(
        per_device,
        mesh=mesh,
        in_specs=(P(("pairs", "tgt"), None), P(("pairs", "tgt"), None, None), P(), P()),
        out_specs=(
            P(("pairs", "tgt"), None, None),
            P(("pairs", "tgt"), None),
            P(("pairs", "tgt"), None),
        ),
        check_vma=False,
    )
```

profile of v0, /device:TPU:0, one launch (start us, length us, event | category | flops | bytes accessed | tf_op | source)
XLA Modules:
  0.0 93.0 jit_solution(4818545377180773034)
XLA Ops:
  7.2 1.7 %fusion.18 = bf16[128,256]{1,0:T(8,128)(2,1)} fusion(bf16[128,128]{1,0:T(8,128)(2,1)} %param.6, bf16[128,256]{1,0:T(8,128)(2,1)} %param.8, f32[256]{0:T(256)} %param.9), kind=kOutput, calls=%fused_computation.23 | convolution fusion | flops 8454144 | bytes 164864 | tf_op jit(solution)/shard_map/dot_general | solution.py:9
  8.9 2.6 %fusion.17 = f32[2048,256]{1,0:T(8,128)} fusion(bf16[2048,128]{1,0:T(8,128)(2,1)S(1)} %bitcast.40, bf16[128,256]{1,0:T(8,128)(2,1)} %param.8, f32[256]{0:T(256)} %param.9), kind=kOutput, calls=%fused_computation.21 | convolution fusion | flops 135790592 | bytes 2688000 | tf_op jit(solution)/shard_map/dot_general | solution.py:9
  11.5 2.5 %reshape.38 = f32[4,2,128,2,256]{4,3,2,1,0:T(2,128)S(1)} reshape(f32[2048,256]{1,0:T(8,128)} %fusion.17) | data formatting | bytes 4194304 | tf_op jit(solution)/shard_map/reshape;reshape | solution.py:15
  14.0 1.5 %reduce_sum.27 = f32[4,128,256]{2,1,0:T(8,128)S(1)} reduce(f32[4,2,128,2,256]{4,3,2,1,0:T(2,128)S(1)} %reshape.38, f32[]{:T(128)} %constant.47.clone.1), dimensions={1,3}, to_apply=%region_0.0 | reduce | flops 393216 | bytes 2621444 | tf_op jit(solution)/shard_map/reduce_sum | solution.py:15
  15.5 0.3 div.27
  15.9 0.4 reduce_sum.28
  16.3 35.1 %all-gather.2.cloned.1.call-done = bf16[2048,256]{1,0:T(8,128)(2,1)} async-done(((bf16[128,256]{1,0:T(8,128)(2,1)}), bf16[2048,256]{1,0:T(8,128)(2,1)}) %all-gather.2.cloned.1.call-update) | async-done | bytes 1048592 | tf_op jit(solution)/shard_map/all_gather | solution.py:45
  51.4 0.9 broadcast_in_dim.9
  52.3 1.6 %broadcast_in_dim.8.clone = bf16[512,2048]{1,0:T(8,128)(2,1)} broadcast(bf16[]{:T(256)} %constant.46.clone.1), dimensions={} | broadcast | bytes 2097154 | tf_op jit(solution)/shard_map/broadcast_in_dim | solution.py:51
  53.9 11.4 %while.15 = (s32[]{:T(128)}, bf16[512,2048]{1,0:T(8,128)(2,1)}, bf16[2048,128]{1,0:T(8,128)(2,1)}, bf16[2048,256]{1,0:T(8,128)(2,1)S(1)}, bf16[512,256]{1,0:T(8,...) while((s32[]{:T(128)}, bf16[512,2048]{1,0:T(8,128)(2,1)}, ...), condition=%wide.region_3.0_spmd, body=%wide.region_2.0_spmd.sunk | while | flops 336527360 | bytes 7079091 | solution.py:81
  54.1 0.9 fusion.52
  55.0 0.3 fusion.49
  55.3 0.3 fusion.50
  55.9 0.8 constant_dynamic-update-slice_fusion.2
  56.9 0.9 fusion.52
  57.8 0.3 fusion.49
  58.2 0.3 fusion.50
  58.7 0.8 constant_dynamic-update-slice_fusion.2
  59.5 0.2 fusion.51
  59.8 0.9 fusion.52
  60.7 0.3 fusion.49
  61.0 0.3 fusion.50
  61.5 0.8 constant_dynamic-update-slice_fusion.2
  62.6 0.9 fusion.52
  63.5 0.3 fusion.49
  63.8 0.3 fusion.50
  64.4 0.8 constant_dynamic-update-slice_fusion.2
  65.2 18.1 %all_to_all.19 = bf16[16,128,128]{2,1,0:T(8,128)(2,1)S(1)} all-to-all(bf16[16,128,128]{2,1,0:T(8,128)(2,1)} %bitcast.5), channel_id=1, replica_groups=mesh['pairs'=2,'tgt'=16] {'tgt'}, dimensions={0} | all-to-all | bytes 1048576 | tf_op jit(solution)/shard_map/all_to_all | solution.py:83
  83.3 0.3 copy.22
  83.6 1.0 %copy.25 = bf16[128,2048]{1,0:T(8,128)(2,1)} copy(bf16[128,2048]{0,1:T(8,128)(2,1)S(1)} %bitcast.44) | data formatting | bytes 1048576
  84.7 0.5 copy.23
  85.4 0.8 copy.26
  (21 shorter events, 1.9 us)
Async XLA Ops:
  7.2 1.8 %copy-start = (bf16[8,256,128]{2,1,0:T(8,128)(2,1)S(1)}, bf16[8,256,128]{2,1,0:T(8,128)(2,1)}, u32[]{:S(2)}) copy-start(bf16[8,256,128]{2,1,0:T(8,128)(2,1)} %param.7) | copy-start | bytes 1572868
  7.2 44.2 %all-gather.2.cloned.1.call-start = ((), (), s32[]{:S(2)}) async-start(), calls=%async_computation.1 | async-start | bytes 1114112 | tf_op jit(solution)/shard_map/all_gather | solution.py:45
  51.4 2.4 %copy-start.1 = (bf16[2048,256]{1,0:T(8,128)(2,1)S(1)}, bf16[2048,256]{1,0:T(8,128)(2,1)}, u32[]{:S(2)}) copy-start(bf16[2048,256]{1,0:T(8,128)(2,1)} %all-gather.2.cloned.1.call-done) | copy-start | bytes 3145732
Sparse Core Ops, SparseCore 0:
  10.8 40.6 all-gather.1
where the time goes:
time: 93.3 us; the launch traced here: 93 us
  waiting for transfers between devices  35.1 us (38%)
  blocking collectives  18.1 us (19%)
  between operations  14.2 us (15%)
  local copies, waits for them, and re-layouts  12 us (13%)
  matrix products  11.3 us (12%)
  other arithmetic  2.17 us (2%)
    all_gather x1, waiting for transfers between devices, per_device(): all_features = lax.all_gather(own_features, 'tgt', axis=0, tiled=True)  35.1 us
    all_to_all x1, blocking collectives, per_device(): lax.all_to_all(coarse_rows, 'tgt', split_axis=0, concat_axis=1, tiled=True)  18.1 us
    dot_general x2, matrix products, project_features(): result = jnp.dot(hidden, weight, preferred_element_type=jnp.float32) + bias  4.25 us
    dynamic_update_slice x8, local copies, waits for them, and re-layouts, one_block(): lax.dynamic_update_slice(level_one, (fine_corr * inverse_root).astype(jnp...  4.19 us
    dot_general x4, matrix products, one_block(): lax.dot_general(panel, coarse_lower, contract_last, preferred_element_typ...  3.57 us
    another operation x1, local copies, waits for them, and re-layouts, pool_leading(): values.reshape(height // 2, 2, across // 2, 2, depth).mean(axis=(1, 3))  2.49 us
  transfers between devices with their start and end apart: 1, of which 1 were waited for; matrix products, arithmetic and copies ran while one was open for 8% of the time, Pallas kernels for 0%

commit v1 on v0

--- a/solution.py
+++ b/solution.py
@@ -42,7 +42,14 @@
     fine_upper, fine_lower = split_parts(fine_pool.reshape(-1, channels))
     coarse_upper, coarse_lower = split_parts(coarse_pool.reshape(-1, channels))
     own_features = project_features(src_hidden, proj_weight, proj_bias)
-    all_features = lax.all_gather(own_features, "tgt", axis=0, tiled=True)
+    ways, here, step = (lax.axis_size("tgt"), lax.axis_index("tgt"), own_features.shape[0])
+    line, have = (own_features, 1)
+    while have < ways:
+        line = jnp.concatenate(
+            [line, lax.ppermute(line, "tgt", [(d, (d - have) % ways) for d in range(ways)])], axis=0
+        )
+        have = 2 * have
+    all_features = jnp.roll(line, here * step, axis=0)
     block_size = 512
     block_total = source_count // block_size
     fine_count = fine_upper.shape[0]

time: 93.3 us -> 89.7 us (0.961)
  between operations: 14.2 us -> 0.88 us
  starting transfers between devices: 0.04 us -> 6.73 us
  blocking collectives: 18.1 us -> 22.3 us
  waiting for transfers between devices: 35.1 us -> 33.4 us
    all_gather x1 -> x0, waiting for transfers between devices: 35.1 us -> none  [per_device(): all_features = lax.all_gather(own_features, 'tgt', axis=0, tiled=True)]
    ppermute x0 -> x4, waiting for transfers between devices: none -> 33.4 us  [per_device(): lax.ppermute(line, 'tgt', [(d, (d - have) % ways) for d in range(ways)])]
    ppermute x0 -> x4, starting transfers between devices: none -> 6.73 us  [per_device(): lax.ppermute(line, 'tgt', [(d, (d - have) % ways) for d in range(ways)])]
    all_to_all x1, blocking collectives: 18.1 us -> 22.3 us  [per_device(): lax.all_to_all(coarse_rows, 'tgt', split_axis=0, concat_axis=1, tiled=True)]
    unnamed x6 -> x14, local copies, waits for them, and re-layouts: 1.8 us -> 1.92 us
  transfers between devices with their start and end apart: 1 -> 4, of which waited for: 1 -> 3; matrix products, arithmetic and copies ran while one was open for 8% -> 8% of each run, Pallas kernels for 0% -> 0%
where the time goes in v1:
time: 89.7 us; the launch traced here: 89.4 us
  waiting for transfers between devices  33.4 us (37%)
  blocking collectives  22.3 us (25%)
  local copies, waits for them, and re-layouts  12.3 us (14%)
  matrix products  11.3 us (13%)
  starting transfers between devices  6.73 us (8%)
  other arithmetic  2.24 us (2%)
    ppermute x4, waiting for transfers between devices, per_device(): lax.ppermute(line, 'tgt', [(d, (d - have) % ways) for d in range(ways)])  33.4 us
    all_to_all x1, blocking collectives, per_device(): lax.all_to_all(coarse_rows, 'tgt', split_axis=0, concat_axis=1, tiled=True)  22.3 us
    ppermute x4, starting transfers between devices, per_device(): lax.ppermute(line, 'tgt', [(d, (d - have) % ways) for d in range(ways)])  6.73 us
    dot_general x2, matrix products, project_features(): result = jnp.dot(hidden, weight, preferred_element_type=jnp.float32) + bias  4.28 us
    dynamic_update_slice x8, local copies, waits for them, and re-layouts, one_block(): lax.dynamic_update_slice(level_one, (fine_corr * inverse_root).astype(jnp...  4.19 us
    dot_general x4, matrix products, one_block(): lax.dot_general(panel, coarse_lower, contract_last, preferred_element_typ...  3.56 us
    another operation x1, local copies, waits for them, and re-layouts, pool_leading(): values.reshape(height // 2, 2, across // 2, 2, depth).mean(axis=(1, 3))  2.49 us
    unnamed x14, local copies, waits for them, and re-layouts  1.92 us
  transfers between devices with their start and end apart: 4, of which 3 were waited for; matrix products, arithmetic and copies ran while one was open for 8% of the time, Pallas kernels for 0%

profile of v1, /device:TPU:0, one launch (start us, length us, event | category | flops | bytes accessed | tf_op | source)
XLA Modules:
  0.0 89.4 jit_solution(491900862904732132)
XLA Ops:
  0.6 1.7 %constant_dynamic-update-slice_fusion.10 = (bf16[4096,256]{1,0:T(8,128)(2,1)}, bf16[128,256]{1,0:T(8,128)(2,1)S(1)}) fusion(f32[256]{0:T(256)} %param.9, bf16[128,128]{1,0:T(8,128)(2,1)} %param.6, bf16[128,256]{1,0:T(8,128)(2,1)} %param.8), kind=kOutput, calls=%fused_computation.45 | convolution fusion | flops 8454143 | bytes 230400 | tf_op jit(solution)/shard_map/dot_general | solution.py:9
  2.3 5.4 %collective-permute-start = (bf16[128,256]{1,0:T(8,128)(2,1)S(1)}, bf16[128,256]{1,0:T(8,128)(2,1)S(1)}, u32[]{:S(2)}, u32[]{:S(2)}) collective-permute-start(bf16[128,256]{1,0:T(8,128)(2,1)S(1)} %get-tuple-element.178), channel_id=1, source_target_pairs={{0,15},{1,0},{2,1},{3,2},{4,3},{5,4},{6,5},{7,6},{8,7},{9,8},{10,9... | collective-permute-start | bytes 196616 | tf_op jit(solution)/shard_map/ppermute | solution.py:49
  7.8 2.6 %fusion.17 = f32[2048,256]{1,0:T(8,128)} fusion(bf16[2048,128]{1,0:T(8,128)(2,1)S(1)} %bitcast.40, bf16[128,256]{1,0:T(8,128)(2,1)} %param.8, f32[256]{0:T(256)} %param.9), kind=kOutput, calls=%fused_computation.21 | convolution fusion | flops 135790592 | bytes 2688000 | tf_op jit(solution)/shard_map/dot_general | solution.py:9
  10.4 2.5 %reshape.38 = f32[4,2,128,2,256]{4,3,2,1,0:T(2,128)S(1)} reshape(f32[2048,256]{1,0:T(8,128)} %fusion.17) | data formatting | bytes 4194304 | tf_op jit(solution)/shard_map/reshape;reshape | solution.py:15
  12.9 1.5 %reduce_sum.27 = f32[4,128,256]{2,1,0:T(8,128)S(1)} reduce(f32[4,2,128,2,256]{4,3,2,1,0:T(2,128)S(1)} %reshape.38, f32[]{:T(128)} %constant.74.clone.1), dimensions={1,3}, to_apply=%region_0.0 | reduce | flops 393216 | bytes 2621444 | tf_op jit(solution)/shard_map/reduce_sum | solution.py:15
  14.4 0.6 collective-permute-start.1
  15.4 0.4 reduce_sum.28
  15.7 3.7 %collective-permute-done.1 = bf16[256,256]{1,0:T(8,128)(2,1)S(1)} collective-permute-done((bf16[256,256]{1,0:T(8,128)(2,1)S(1)}, bf16[256,256]{1,0:T(8,128)(2,1)S(1)}, u32[]{:S(2)}, u32[]{:S(2)}) %collective-permute-start.1) | collective-permute-done | bytes 131104 | tf_op jit(solution)/shard_map/ppermute | solution.py:49
  19.4 0.6 collective-permute-start.2
  20.1 6.3 %collective-permute-done.2 = bf16[512,256]{1,0:T(8,128)(2,1)S(1)} collective-permute-done((bf16[512,256]{1,0:T(8,128)(2,1)S(1)}, bf16[512,256]{1,0:T(8,128)(2,1)S(1)}, u32[]{:S(2)}, u32[]{:S(2)}) %collective-permute-start.2) | collective-permute-done | bytes 262176 | tf_op jit(solution)/shard_map/ppermute | solution.py:49
  26.7 23.4 %collective-permute-done.3 = bf16[1024,256]{1,0:T(8,128)(2,1)S(1)} collective-permute-done((bf16[1024,256]{1,0:T(8,128)(2,1)S(1)}, bf16[1024,256]{1,0:T(8,128)(2,1)S(1)}, u32[]{:S(2)}, u32[]{:S(2)}) %collective-permute-start.3) | collective-permute-done | bytes 524320 | tf_op jit(solution)/shard_map/ppermute | solution.py:49
  50.3 1.6 %broadcast_in_dim.8.clone = bf16[512,2048]{1,0:T(8,128)(2,1)} broadcast(bf16[]{:T(256)} %constant.68.clone.1), dimensions={} | broadcast | bytes 2097154 | tf_op jit(solution)/shard_map/broadcast_in_dim | solution.py:58
  51.9 0.9 broadcast_in_dim.9
  52.8 11.4 %while.15 = (s32[]{:T(128)}, bf16[512,2048]{1,0:T(8,128)(2,1)}, bf16[2048,128]{1,0:T(8,128)(2,1)}, bf16[2048,256]{1,0:T(8,128)(2,1)S(1)}, bf16[512,256]{1,0:T(8,...) while((s32[]{:T(128)}, bf16[512,2048]{1,0:T(8,128)(2,1)}, ...), condition=%wide.region_3.4_spmd, body=%wide.region_2.3_spmd.sunk | while | flops 336527360 | bytes 7079091 | solution.py:88
  52.8 0.3 fusion.49
  53.1 0.3 fusion.50
  53.7 0.8 constant_dynamic-update-slice_fusion.12
  54.7 0.9 fusion.52
  56.0 0.3 fusion.50
  56.5 0.8 constant_dynamic-update-slice_fusion.12
  57.6 0.9 fusion.52
  58.5 0.3 fusion.49
  58.8 0.3 fusion.50
  59.3 0.8 constant_dynamic-update-slice_fusion.12
  60.4 0.9 fusion.52
  61.6 0.3 fusion.50
  62.2 0.8 constant_dynamic-update-slice_fusion.12
  63.2 0.9 fusion.52
  64.1 22.3 %all_to_all.19 = bf16[16,128,128]{2,1,0:T(8,128)(2,1)S(1)} all-to-all(bf16[16,128,128]{2,1,0:T(8,128)(2,1)} %bitcast.44), channel_id=1, replica_groups=mesh['pairs'=2,'tgt'=16] {'tgt'}, dimensions={0} | all-to-all | bytes 1048576 | tf_op jit(solution)/shard_map/all_to_all | solution.py:90
  86.6 0.5 copy.23
  87.3 0.8 copy.26
  88.3 1.0 %copy.25 = bf16[128,2048]{1,0:T(8,128)(2,1)} copy(bf16[128,2048]{0,1:T(8,128)(2,1)S(1)} %bitcast.45) | data formatting | bytes 1048576
  (39 shorter events, 3.7 us)
Async XLA Ops:
  0.6 7.1 %copy-start = (bf16[8,256,128]{2,1,0:T(8,128)(2,1)S(1)}, bf16[8,256,128]{2,1,0:T(8,128)(2,1)}, u32[]{:S(2)}) copy-start(bf16[8,256,128]{2,1,0:T(8,128)(2,1)} %param.7) | copy-start | bytes 1572868
  2.3 12.0 %collective-permute-start = (bf16[128,256]{1,0:T(8,128)(2,1)S(1)}, bf16[128,256]{1,0:T(8,128)(2,1)S(1)}, u32[]{:S(2)}, u32[]{:S(2)}) collective-permute-start(bf16[128,256]{1,0:T(8,128)(2,1)S(1)} %get-tuple-element.178), channel_id=1, source_target_pairs={{0,15},{1,0},{2,1},{3,2},{4,3},{5,4},{6,5},{7,6},{8,7},{9,8},{10,9... | collective-permute-start | bytes 196616 | tf_op jit(solution)/shard_map/ppermute | solution.py:49
  14.4 5.0 %collective-permute-start.1 = (bf16[256,256]{1,0:T(8,128)(2,1)S(1)}, bf16[256,256]{1,0:T(8,128)(2,1)S(1)}, u32[]{:S(2)}, u32[]{:S(2)}) collective-permute-start(bf16[256,256]{1,0:T(8,128)(2,1)S(1)} %pad_maximum_fusion.2), channel_id=1, source_target_pairs={{0,14},{1,15},{2,0},{3,1},{4,2},{5,3},{6,4},{7,5},{8,6},{9,7},{10,... | collective-permute-start | bytes 393224 | tf_op jit(solution)/shard_map/ppermute | solution.py:49
  19.4 7.0 %collective-permute-start.2 = (bf16[512,256]{1,0:T(8,128)(2,1)S(1)}, bf16[512,256]{1,0:T(8,128)(2,1)S(1)}, u32[]{:S(2)}, u32[]{:S(2)}) collective-permute-start(bf16[512,256]{1,0:T(8,128)(2,1)S(1)} %pad_maximum_fusion.1), channel_id=1, source_target_pairs={{0,12},{1,13},{2,14},{3,15},{4,0},{5,1},{6,2},{7,3},{8,4},{9,5},{1... | collective-permute-start | bytes 786440 | tf_op jit(solution)/shard_map/ppermute | solution.py:49
  20.1 6.5 %copy-start.1 = (bf16[4096,256]{1,0:T(8,128)(2,1)S(1)}, bf16[4096,256]{1,0:T(8,128)(2,1)}, u32[]{:S(2)}) copy-start(bf16[4096,256]{1,0:T(8,128)(2,1)} %get-tuple-element.177) | copy-start | bytes 6291460
  26.5 23.6 %collective-permute-start.3 = (bf16[1024,256]{1,0:T(8,128)(2,1)S(1)}, bf16[1024,256]{1,0:T(8,128)(2,1)S(1)}, u32[]{:S(2)}, u32[]{:S(2)}) collective-permute-start(bf16[1024,256]{1,0:T(8,128)(2,1)S(1)} %pad_maximum_fusion), channel_id=1, source_target_pairs={{0,8},{1,9},{2,10},{3,11},{4,12},{5,13},{6,14},{7,15},{8,0},{9,1},... | collective-permute-start | bytes 1572872 | tf_op jit(solution)/shard_map/ppermute | solution.py:49
